TPU v7x, 512 devices: a whole 4x8x8 slice. The times are simulated.
512 devices in a mesh: row: 16 (over y_hi, x), col: 32 (over z, y_lo, core).
Axes of the slice: x: 4, y: 8 (y_hi: 4, y_lo: 2; y = y_hi * 2 + y_lo), z: 8, core: 2. Of those that a mesh axis runs over, the one named last changes fastest.
Arguments:
- panel_factor: bfloat16 [128, 20480], P('row', 'col'), may hold values from -0.5 to 0.5
- diag_inverse: bfloat16 [128, 128], P('col'), may hold values from -0.5 to 0.5
- panel_rhs: bfloat16 [128, 18432], P('col', 'row'), may hold values from -6 to 6
- trail_rhs: bfloat16 [18432, 20480], P('row', 'col'), may hold values from -6 to 6
- forward_field: bfloat16 [18432, 20480], P('row', 'col'), may hold values from -6 to 6
- pivot: int32 [128], replicated, may hold values from 0 to 127, each once
- panel_harmonic: int32 [2, 128], replicated, may hold values from 0 to 90
- trail_harmonic: int32 [2, 20480], P(None, 'col'), may hold values from 0 to 90
Outputs:
- panel_adjoint: bfloat16 [128, 18432], P(None, 'row')
- trail_update: bfloat16 [18432, 20480], P('row', 'col')
- eps_grad: float32 [36864], P(('row', 'col'))
All inputs are finite; a program needn't handle non-finite values.
Results may differ from a plain program's by a relative error of at most 0.0039.
Values may be sent and summed in bfloat16 or wider, within the bound.
A program may use at most 64 MiB of HBM per device.

v0:
```python
import math

import jax
import jax.numpy as jnp
from jax import lax
from jax.sharding import Mesh
from jax.sharding import PartitionSpec as P

NB = 128
S = 18432
ORDERS = 91
DPITCH = 192
NDIAG = 36864
COL = ("col_0", "col_1", "col_2")
ROW = ("row_0", "row_1")
ROW_COL = ("row_0", "row_1", "col_0", "col_1", "col_2")


def in_one_piece(arrays, axis, dim, along):
    widths = [a.shape[along] for a in arrays]
    both = jnp.concatenate(arrays, axis=along)
    result = lax.all_gather(both, axis, axis=dim, tiled=True)
    return tuple(jnp.split(result, [sum(widths[:k]) for k in range(1, len(widths))], axis=along))


def sent_to_all(array, axis):
    copies = jnp.broadcast_to(array, (lax.axis_size(axis), *array.shape))
    return lax.all_to_all(copies, axis, split_axis=0, concat_axis=0, tiled=True)


def in_order(tiles, dim):
    dims = list(tiles.shape[1:])
    dims[dim] *= tiles.shape[0]
    return jnp.moveaxis(tiles, 0, dim).reshape(dims)


def collect(array, axis, dim):
    tiles = sent_to_all(array, axis)
    return in_order(tiles, dim)


def cut_along(array, dim, devices):
    before, after = (array.shape[:dim], array.shape[dim + 1 :])
    return jnp.moveaxis(array.reshape(*before, devices, -1, *after), dim, 0)


def summed_on_arrival(array, axis, dim):
    tiles = cut_along(array, dim, lax.axis_size(axis))
    arrived = lax.all_to_all(tiles, axis, split_axis=0, concat_axis=0, tiled=True)
    return arrived.sum(axis=0)


def sum_by_chip(array, chips, core, dim):
    sizes = (lax.axis_size(chips), lax.axis_size(core))
    tiles = cut_along(array, dim, sizes[0] * sizes[1])
    inside = tiles.shape[1:]
    tiles = tiles.reshape(*sizes, *inside).swapaxes(0, 1).reshape(-1, *inside)
    tiles = lax.psum_scatter(tiles, core, scatter_dimension=0, tiled=True)
    return lax.psum_scatter(tiles, chips, scatter_dimension=0, tiled=True)[0]


def per_device(
    panel_factor,
    diag_inverse,
    panel_rhs,
    trail_rhs,
    forward_field,
    pivot,
    panel_harmonic,
    trail_harmonic,
):
    contract_first = (((0,), (0,)), ((), ()))
    inverse_all, rhs_all = in_one_piece((diag_inverse, panel_rhs), COL, 0, 1)
    panel_adjoint = lax.dot_general(
        inverse_all, rhs_all, contract_first, preferred_element_type=jnp.float32
    ).astype(jnp.bfloat16)
    update = lax.dot_general(
        panel_adjoint,
        collect(panel_factor, ROW, 0),
        contract_first,
        preferred_element_type=jnp.float32,
    )
    trail_update = (trail_rhs.astype(jnp.float32) - update).astype(jnp.bfloat16)
    correlation = jnp.dot(panel_adjoint, forward_field, preferred_element_type=jnp.float32)
    harmonic_rows = panel_harmonic[:, pivot]
    correlation = summed_on_arrival(correlation, ROW, 0)
    row_count = NB // lax.axis_size(ROW)
    first_row = lax.axis_index(ROW) * row_count
    harmonic_rows = lax.dynamic_slice_in_dim(harmonic_rows, first_row, row_count, 1)
    delta_x = harmonic_rows[0][:, None] - trail_harmonic[0][None, :] + (ORDERS - 1)
    delta_y = harmonic_rows[1][:, None] - trail_harmonic[1][None, :] + (ORDERS - 1)
    cell_index = (delta_x * DPITCH + delta_y).reshape(-1)
    partial_grad = jax.ops.segment_sum(correlation.reshape(-1), cell_index, num_segments=NDIAG)
    gradient = sum_by_chip(partial_grad, ("row_0", "row_1", "col_0", "col_1"), "col_2", 0)
    eps_grad = gradient * jnp.float32(1.0 / math.sqrt(S * NB))
    return (panel_adjoint, trail_update, eps_grad)


def solution(mesh):
    torus = Mesh(mesh.devices.reshape(4, 4, 8, 2, 2), ("row_0", "row_1", "col_0", "col_1", "col_2"))
    placed = (
        P(ROW, COL),
        P(COL, None),
        P(COL, ROW),
        P(ROW, COL),
        P(ROW, COL),
        P(),
        P(),
        P(None, COL),
    )
    return jax.shard_map(
        per_device,
        mesh=torus,
        in_specs=placed,
        out_specs=(P(None, ROW), P(ROW, COL), P(ROW_COL)),
        check_vma=False,
    )
```

profile of v0, /device:TPU:1, one launch (start us, length us, event | category | flops | bytes accessed | tf_op | source)
XLA Modules:
  0.0 363.7 jit_solution(15242929018980873267)
XLA Ops:
  7.2 0.8 maximum_bitcast_fusion
  8.0 43.1 %all-gather = bf16[32,4,1280]{2,1,0:T(4,128)(2,1)S(1)} all-gather(bf16[1,4,1280]{2,1,0:T(4,128)(2,1)S(1)} %maximum_bitcast_fusion), channel_id=1, replica_groups=mesh['row_0'=4,'row_1'=4,'col_0'=8,'col_1'=2,'col_2'=2] {'col_0','col_1'..., dimensions={0}, use_global_device_ids=true | all-gather | bytes 337920 | tf_op jit(solution)/shard_map/all_gather | solution.py:22
  51.1 0.1 reshape.108
  51.1 0.3 convolution_convert_fusion
  51.5 1.1 convolution_bitcast_fusion
  52.6 8.5 %all-to-all-start.1 = ((f32[16,8,640]{2,1,0:T(8,128)}), f32[16,8,640]{2,1,0:T(8,128)}, u32[]{:S(2)}, u32[]{:S(2)}) async-start(f32[16,8,640]{2,1,0:T(8,128)} %convolution_bitcast_fusion), calls=%async_computation.1 | async-start | bytes 655360 | tf_op jit(solution)/shard_map/all_to_all | solution.py:49
  61.2 0.1 copy.17
  61.3 0.6 gather_fusion
  62.0 0.2 slice_reduce_fusion.1
  62.2 12.3 %all-to-all-done.1 = f32[16,8,640]{2,1,0:T(8,128)} async-done(((f32[16,8,640]{2,1,0:T(8,128)}), f32[16,8,640]{2,1,0:T(8,128)}, u32[]{:S(2)}, u32[]{:S(2)}) %all-to-all-start.1) | async-done | bytes 327712 | tf_op jit(solution)/shard_map/all_to_all | solution.py:49
  74.5 0.7 broadcast_in_dim.9
  75.2 4.2 %all-to-all-start = ((bf16[16,8,640]{2,1,0:T(8,128)(2,1)}), bf16[16,8,640]{2,1,0:T(8,128)(2,1)}, u32[]{:S(2)}, u32[]{:S(2)}) async-start(bf16[16,8,640]{2,1,0:T(8,128)(2,1)} %broadcast_in_dim.9), calls=%async_computation | async-start | bytes 327680 | tf_op jit(solution)/shard_map/all_to_all | solution.py:28
  79.4 0.0 reduce-scatter.3.cloned.1.call-start
  79.4 0.1 add_add_fusion
  79.5 1.0 reduce_sum.9
  80.5 27.8 %scatter_custom_fusion = f32[36864]{0:T(1024)} fusion(s32[5120]{0:T(1024)S(1)} %reshape.99, f32[5120]{0:T(1024)S(1)} %reshape.101, f32[]{:T(128)} %constant.11.clone.1), kind=kCustom, calls=%fused_computation.8 | custom fusion | flops 5120 | bytes 147460 | tf_op jit(solution)/shard_map/scatter-add | solution.py:93
  108.4 1.4 reshape_reshape.3
  109.8 0.8 copy.18
  110.6 1.6 copy.21
  112.2 1.3 dynamic-slice.1
  113.6 12.9 %reduce-scatter.3.cloned.1.call-done = f32[256,72]{0,1:T(8,128)} async-done(((f32[512,72]{0,1:T(8,128)}), f32[256,72]{0,1:T(8,128)}) %reduce-scatter.3.cloned.1.call-update) | async-done | bytes 73744 | tf_op jit(solution)/shard_map/reduce_scatter | solution.py:58
  126.6 2.6 fusion
  129.2 225.5 %all-reduce.3.cloned.1.call-done = f32[256,72]{0,1:T(8,128)} async-done(((f32[256,72]{0,1:T(8,128)}), f32[256,72]{0,1:T(8,128)}) %all-reduce.3.cloned.1.call-update) | async-done | bytes 73744
  354.7 2.2 fusion.5
  (24 shorter events, 0.2 us)
Async XLA Ops:
  7.2 44.2 %copy-start = (bf16[1152,640]{1,0:T(8,128)(2,1)S(1)}, bf16[1152,640]{1,0:T(8,128)(2,1)}, u32[]{:S(2)}) copy-start(bf16[1152,640]{1,0:T(8,128)(2,1)} %param.12) | copy-start | bytes 4423684
  51.4 75.1 %copy-start.1 = (bf16[128,1152]{1,0:T(8,128)(2,1)}, bf16[128,1152]{1,0:T(8,128)(2,1)S(1)}, u32[]{:S(2)}) copy-start(bf16[128,1152]{1,0:T(8,128)(2,1)S(1)} %convolution_convert_fusion) | copy-start | bytes 884740
  51.4 9.8 %copy-start.5 = (s32[2,128]{1,0:T(2,128)S(1)}, s32[2,128]{1,0:T(2,128)}, u32[]{:S(2)}) copy-start(s32[2,128]{1,0:T(2,128)} %param.14) | copy-start | bytes 3076
  51.4 9.9 %copy-start.6 = (s32[128]{0:T(128)S(1)}, s32[128]{0:T(128)}, u32[]{:S(2)}) copy-start(s32[128]{0:T(128)} %param.13) | copy-start | bytes 1540
  51.5 10.7 %copy-start.4 = (s32[2,640]{1,0:T(2,128)S(1)}, s32[2,640]{1,0:T(2,128)}, u32[]{:S(2)}) copy-start(s32[2,640]{1,0:T(2,128)} %param.15) | copy-start | bytes 15364
  51.5 23.1 %copy-start.3 = (bf16[8,640]{1,0:T(8,128)(2,1)S(1)}, bf16[8,640]{1,0:T(8,128)(2,1)}, u32[]{:S(2)}) copy-start(bf16[8,640]{1,0:T(8,128)(2,1)} %param.8) | copy-start | bytes 30724
  52.6 21.9 %all-to-all-start.1 = ((f32[16,8,640]{2,1,0:T(8,128)}), f32[16,8,640]{2,1,0:T(8,128)}, u32[]{:S(2)}, u32[]{:S(2)}) async-start(f32[16,8,640]{2,1,0:T(8,128)} %convolution_bitcast_fusion), calls=%async_computation.1 | async-start | bytes 655360 | tf_op jit(solution)/shard_map/all_to_all | solution.py:49
  61.2 65.4 %copy-start.2 = (bf16[1152,640]{1,0:T(8,128)(2,1)S(1)}, bf16[1152,640]{1,0:T(8,128)(2,1)}, u32[]{:S(2)}) copy-start(bf16[1152,640]{1,0:T(8,128)(2,1)} %param.11) | copy-start | bytes 4423684
  75.2 51.3 %all-to-all-start = ((bf16[16,8,640]{2,1,0:T(8,128)(2,1)}), bf16[16,8,640]{2,1,0:T(8,128)(2,1)}, u32[]{:S(2)}, u32[]{:S(2)}) async-start(bf16[16,8,640]{2,1,0:T(8,128)(2,1)} %broadcast_in_dim.9), calls=%async_computation | async-start | bytes 327680 | tf_op jit(solution)/shard_map/all_to_all | solution.py:28
  79.4 47.1 %reduce-scatter.3.cloned.1.call-start = ((), (), s32[]{:S(2)}) async-start(), calls=%async_computation.3 | async-start | bytes 221184 | tf_op jit(solution)/shard_map/reduce_scatter | solution.py:58
  112.2 242.5 %all-reduce.3.cloned.1.call-start = ((), (), s32[]{:S(2)}) async-start(), calls=%async_computation.4 | async-start | bytes 147456
Sparse Core Ops, SparseCore 0:
  112.3 14.1 reduce-scatter.2
  131.4 223.2 all-reduce.2
where the time goes:
time: 367 us; the launch traced here: 364 us
  waiting for transfers between devices  251 us (68%)
  blocking collectives  43.1 us (12%)
  other arithmetic  31.9 us (9%)
  between operations  14.2 us (4%)
  starting transfers between devices  12.8 us (3%)
  local copies, waits for them, and re-layouts  6.9 us (2%)
  matrix products  4 us (1%)
    unnamed x3, waiting for transfers between devices  226 us
    all_gather x1, blocking collectives, in_one_piece(): result = lax.all_gather(both, axis, axis=dim, tiled=True)  43.1 us
    scatter-add x1, other arithmetic, per_device(): jax.ops.segment_sum(correlation.reshape(-1), cell_index, num_segments=NDIAG)  27.8 us
    reduce_scatter x1, waiting for transfers between devices, sum_by_chip(): tiles = lax.psum_scatter(tiles, core, scatter_dimension=0, tiled=True)  12.9 us
    all_to_all x1, waiting for transfers between devices, summed_on_arrival(): lax.all_to_all(tiles, axis, split_axis=0, concat_axis=0, tiled=True)  12.3 us
    all_to_all x1, starting transfers between devices, summed_on_arrival(): lax.all_to_all(tiles, axis, split_axis=0, concat_axis=0, tiled=True)  8.54 us
  transfers between devices with their start and end apart: 4, of which 3 were waited for; matrix products, arithmetic and copies ran while one was open for 10% of the time, Pallas kernels for 0%

commit v1 on v0

v1 whole, which is shorter than its diff:
```python
import functools
import math

import jax
import jax.numpy as jnp
from jax import lax
from jax.experimental import pallas as pl
from jax.experimental.pallas import tpu as pltpu
from jax.sharding import PartitionSpec as P

NB = 128
S = 18432
NR = 16
NC = 32
SB = 1152
QB = 640
HALF = 640
MESH = pl.DeviceIdType.MESH
BF = jnp.bfloat16
F32 = jnp.float32


def kernel(
    pf_hbm, dinv_hbm, rhs_hbm, trail_hbm, ff_hbm, piv_hbm, ph_hbm, th_hbm,
    pa_out, tu_out, eps_out,
    pf_v, raw, trail_v, ff_v, th_v, piv_s, ph_s,
    stage, a_land, b_land, pa, corr, c_send, c_land, hot, u_x, g_send, d_land, h_lo, h_hi, e_send, e_land,
    loc, sems,
):
    row = lax.axis_index("row")
    col = lax.axis_index("col")
    core = col % 2

    def row_peer(k):
        return (row + k) % NR

    def col_peer(k):
        return (col + k) % NC

    copies = [
        pltpu.make_async_copy(rhs_hbm, raw.at[:, pl.ds(0, SB)], loc.at[0]),
        pltpu.make_async_copy(dinv_hbm, raw.at[:, pl.ds(SB, NB)], loc.at[1]),
        pltpu.make_async_copy(pf_hbm, pf_v, loc.at[2]),
        pltpu.make_async_copy(th_hbm, th_v, loc.at[3]),
        pltpu.make_async_copy(piv_hbm, piv_s, loc.at[4]),
        pltpu.make_async_copy(ph_hbm, ph_s, loc.at[5]),
        pltpu.make_async_copy(ff_hbm, ff_v, loc.at[6]),
        pltpu.make_async_copy(trail_hbm, trail_v, loc.at[7]),
    ]
    for c in copies:
        c.start()

    barrier = pltpu.get_barrier_semaphore()

    @pl.loop(1, NC)
    def _(k):
        pl.semaphore_signal(barrier, inc=1, device_id=(row, col_peer(k)), device_id_type=MESH)

    @pl.loop(1, NR)
    def _(k):
        pl.semaphore_signal(barrier, inc=1, device_id=(row_peer(k), col), device_id_type=MESH)

    copies[0].wait()
    copies[1].wait()
    stage[0, :, pl.ds(0, HALF)] = raw[:, pl.ds(0, HALF)]
    stage[1, :, pl.ds(0, HALF)] = raw[:, pl.ds(SB - HALF, HALF)]
    for h in range(2):
        stage[h, :, pl.ds(HALF, NB)] = raw[:, pl.ds(SB, NB)]
    copies[2].wait()

    pl.semaphore_wait(barrier, NC - 1 + NR - 1)

    def col_copy(src, dst, target, k):
        return pltpu.make_async_remote_copy(
            src_ref=src, dst_ref=dst, send_sem=sems.at[2 * k], recv_sem=sems.at[2 * k + 1],
            device_id=(row, target), device_id_type=MESH,
        )

    def row_copy(src, dst, target, k):
        return pltpu.make_async_remote_copy(
            src_ref=src, dst_ref=dst, send_sem=sems.at[2 * k], recv_sem=sems.at[2 * k + 1],
            device_id=(target, col), device_id_type=MESH,
        )

    @pl.loop(1, NC)
    def _(k):
        target = col_peer(k)
        col_copy(stage.at[target % 2], a_land.at[col], target, 0).start()

    @pl.loop(1, NR)
    def _(k):
        row_copy(pf_v, b_land.at[row], row_peer(k), 1).start()

    a_land[col] = stage[core]
    b_land[row] = pf_v[...]
    c_land[row] = jnp.zeros((8, QB), BF)

    for c in copies[3:6]:
        c.wait()
    hx_q = th_v[pl.ds(0, 1), :]
    hy_q = th_v[pl.ds(1, 1), :]
    u_x[...] = (lax.broadcasted_iota(jnp.int32, (192, QB), 0) + hx_q - 90).astype(BF)
    hy_c = jnp.transpose(jnp.broadcast_to(hy_q.astype(F32), (128, QB)))
    hy_c = jnp.concatenate([hy_c, hy_c], axis=1).astype(jnp.int32)
    u_y = (lax.broadcasted_iota(jnp.int32, (QB, 256), 1) + hy_c - 90).astype(BF)
    hx_a = []
    for j in range(8):
        unpivoted = piv_s[row * 8 + j]
        hx_a.append(ph_s[0, unpivoted].astype(F32).astype(BF))
        hy = ph_s[1, unpivoted].astype(F32).astype(BF)
        hot[pl.ds(j * QB, QB), :] = jnp.where(u_y == hy, jnp.ones((), BF), jnp.zeros((), BF))

    col_copy(a_land.at[pl.ds(0, NC - 1)], a_land.at[pl.ds(0, NC - 1)], col_peer(1), 0).wait_recv()
    both = a_land[...].astype(F32).reshape(NB, HALF + NB).astype(BF)
    mine = lax.dot_general(
        both[:, HALF:], both[:, :HALF], (((0,), (0,)), ((), ())), preferred_element_type=F32
    ).astype(BF)
    pa[:, pl.ds(pl.multiple_of(core * (SB - HALF), 128), HALF)] = mine
    part = pa.at[:, pl.ds(pl.multiple_of(core * HALF, 128), SB - HALF)]
    swap = col_copy(part, part, col + 1 - 2 * core, 2)
    swap.start()
    copies[6].wait()
    swap.wait()

    corr[...] = jnp.dot(pa[...], ff_v[...], preferred_element_type=F32)
    c_send[...] = corr[...].reshape(NR, 8, QB).astype(BF)

    @pl.loop(1, NR)
    def _(k):
        target = row_peer(k)
        row_copy(c_send.at[target], c_land.at[row], target, 3).start()

    row_copy(b_land.at[pl.ds(0, NR - 1)], b_land.at[pl.ds(0, NR - 1)], row_peer(1), 1).wait_recv()
    factor = b_land[...].astype(F32).reshape(NB, QB).astype(BF)
    copies[7].wait()
    for t in range(3):
        at = pl.ds(t * 384, 384)
        update = lax.dot_general(
            pa[:, at], factor, (((0,), (0,)), ((), ())), preferred_element_type=F32
        )
        tu_out[at, :] = (trail_v[at, :].astype(F32) - update).astype(BF)
    pa_out[...] = pa[...]

    row_copy(c_land.at[pl.ds(0, NR - 1)], c_land.at[pl.ds(0, NR - 1)], row_peer(1), 3).wait_recv()
    total = corr[pl.ds(pl.multiple_of(row * 8, 8), 8), :]
    for r in range(NR):
        total = total + c_land[r].astype(F32)
    high = total.astype(BF)
    low = (total - high.astype(F32)).astype(BF)
    grid = jnp.zeros((384, 256), F32)
    for s in range(2):
        pieces = []
        for j in range(4 * s, 4 * s + 4):
            at_x = u_x[...] == hx_a[j]
            pieces.append(
                jnp.concatenate(
                    [
                        jnp.where(at_x, high[j : j + 1, :], jnp.zeros((), BF)),
                        jnp.where(at_x, low[j : j + 1, :], jnp.zeros((), BF)),
                    ],
                    axis=0,
                )
            )
        grid = grid + jnp.dot(
            jnp.concatenate(pieces, axis=1), hot[pl.ds(s * 4 * QB, 4 * QB), :], preferred_element_type=F32
        )
    grid = grid[:192] + grid[192:]
    for r in range(NR):
        g_send[r] = grid[12 * r : 12 * r + 12]

    @pl.loop(1, NR)
    def _(k):
        target = row_peer(k)
        row_copy(g_send.at[target], d_land.at[row], target, 4).start()

    d_land[row] = g_send[row]
    row_copy(d_land.at[pl.ds(0, NR - 1)], d_land.at[pl.ds(0, NR - 1)], row_peer(1), 4).wait_recv()
    summed = d_land[0]
    for r in range(1, NR):
        summed = summed + d_land[r]
    h_lo[...] = summed[:, :128]
    h_hi[...] = summed[:, 128:]

    flat = jnp.concatenate(
        [piece for t in range(3) for piece in (h_lo[pl.ds(t, 4, 3), :], h_hi[pl.ds(t, 4, 3), :][:, :64])], axis=1
    )
    for h in range(8):
        piece = jnp.concatenate([flat[:, 72 * h : 72 * h + 72], jnp.zeros((4, 56), F32)], axis=1)
        for g in range(4):
            e_send[8 * g + h] = piece[g : g + 1]

    @pl.loop(1, NC)
    def _(k):
        target = col_peer(k)
        col_copy(e_send.at[target], e_land.at[col], target, 5).start()

    e_land[col] = e_send[col]
    col_copy(e_land.at[pl.ds(0, NC - 1)], e_land.at[pl.ds(0, NC - 1)], col_peer(1), 5).wait_recv()
    eps_out[...] = jnp.sum(e_land[...], axis=0) * F32(1.0 / math.sqrt(S * NB))

    col_copy(a_land.at[pl.ds(0, NC - 1)], a_land.at[pl.ds(0, NC - 1)], col_peer(1), 0).wait_send()
    row_copy(b_land.at[pl.ds(0, NR - 1)], b_land.at[pl.ds(0, NR - 1)], row_peer(1), 1).wait_send()
    row_copy(c_land.at[pl.ds(0, NR - 1)], c_land.at[pl.ds(0, NR - 1)], row_peer(1), 3).wait_send()
    row_copy(d_land.at[pl.ds(0, NR - 1)], d_land.at[pl.ds(0, NR - 1)], row_peer(1), 4).wait_send()
    col_copy(e_land.at[pl.ds(0, NC - 1)], e_land.at[pl.ds(0, NC - 1)], col_peer(1), 5).wait_send()


def per_device(*args):
    anywhere = pl.BlockSpec(memory_space=pl.ANY)
    vmem = pl.BlockSpec(memory_space=pltpu.VMEM)
    pa, tu, eps = pl.pallas_call(
        kernel,
        out_shape=(
            jax.ShapeDtypeStruct((NB, SB), BF),
            jax.ShapeDtypeStruct((SB, QB), BF),
            jax.ShapeDtypeStruct((1, 128), F32),
        ),
        in_specs=[anywhere] * 8,
        out_specs=(vmem, vmem, vmem),
        scratch_shapes=[
            pltpu.VMEM((8, QB), BF),
            pltpu.VMEM((4, SB + NB), BF),
            pltpu.VMEM((SB, QB), BF),
            pltpu.VMEM((SB, QB), BF),
            pltpu.VMEM((2, QB), jnp.int32),
            pltpu.SMEM((NB,), jnp.int32),
            pltpu.SMEM((2, NB), jnp.int32),
            pltpu.VMEM((2, 4, HALF + NB), BF),
            pltpu.VMEM((NC, 4, HALF + NB), BF),
            pltpu.VMEM((NR, 8, QB), BF),
            pltpu.VMEM((NB, SB), BF),
            pltpu.VMEM((NB, QB), F32),
            pltpu.VMEM((NR, 8, QB), BF),
            pltpu.VMEM((NR, 8, QB), BF),
            pltpu.VMEM((8 * QB, 256), BF),
            pltpu.VMEM((192, QB), BF),
            pltpu.VMEM((NR, 12, 256), F32),
            pltpu.VMEM((NR, 12, 256), F32),
            pltpu.VMEM((12, 128), F32),
            pltpu.VMEM((12, 128), F32),
            pltpu.VMEM((NC, 1, 128), F32),
            pltpu.VMEM((NC, 1, 128), F32),
            pltpu.SemaphoreType.DMA((8,)),
            pltpu.SemaphoreType.DMA((12,)),
        ],
        compiler_params=pltpu.CompilerParams(
            collective_id=0, has_side_effects=True, vmem_limit_bytes=40 * 2**20
        ),
    )(*args)
    return pa, tu, eps[0, :72]


def solution(mesh):
    placed = (
        P("row", "col"),
        P("col", None),
        P("col", "row"),
        P("row", "col"),
        P("row", "col"),
        P(),
        P(),
        P(None, "col"),
    )
    return jax.shard_map(
        per_device,
        mesh=mesh,
        in_specs=placed,
        out_specs=(P(None, "row"), P("row", "col"), P(("row", "col"))),
        check_vma=False,
    )
```

time: 367 us -> 59.2 us (0.16)
  waiting for transfers between devices: 251 us -> 0 us
  Pallas kernels: 0 us -> 49 us
  blocking collectives: 43.1 us -> 0 us
  other arithmetic: 31.9 us -> 0 us
  between operations: 14.2 us -> 0.66 us
  starting transfers between devices: 12.8 us -> 0 us
  matrix products: 4 us -> 0 us
    unnamed x3 -> x0, waiting for transfers between devices: 226 us -> none
    pallas_call x0 -> x1, Pallas kernels: none -> 49 us  [per_device(): pl.pallas_call(kernel, out_shape=(jax.ShapeDtypeStruct((NB, SB), BF), jax...]
    all_gather x1 -> x0, blocking collectives: 43.1 us -> none  [in_one_piece(): result = lax.all_gather(both, axis, axis=dim, tiled=True)]
    scatter-add x1 -> x0, other arithmetic: 27.8 us -> none  [per_device(): jax.ops.segment_sum(correlation.reshape(-1), cell_index, num_segments=NDIAG)]
    reduce_scatter x1 -> x0, waiting for transfers between devices: 12.9 us -> none  [sum_by_chip(): tiles = lax.psum_scatter(tiles, core, scatter_dimension=0, tiled=True)]
    all_to_all x2 -> x0, starting transfers between devices: 12.7 us -> none  [the longest x1 8.54 us: summed_on_arrival(): lax.all_to_all(tiles, axis, split_axis=0, concat_axis=0, tiled=True)]
    all_to_all x2 -> x0, waiting for transfers between devices: 12.3 us -> none  [the longest x1 12.3 us: summed_on_arrival(): lax.all_to_all(tiles, axis, split_axis=0, concat_axis=0, tiled=True)]
    unnamed x18, local copies, waits for them, and re-layouts: 3.16 us -> 8.66 us
  transfers between devices with their start and end apart: 4 -> 0, of which waited for: 3 -> 0; matrix products, arithmetic and copies ran while one was open for 10% -> 0% of each run, Pallas kernels for 0% -> 0%
where the time goes in v1:
time: 59.2 us; the launch traced here: 58.9 us
  Pallas kernels  49 us (83%)
  local copies, waits for them, and re-layouts  9.18 us (16%)
  between operations  0.66 us (1%)
    pallas_call x1, Pallas kernels, per_device(): pl.pallas_call(kernel, out_shape=(jax.ShapeDtypeStruct((NB, SB), BF), jax...  49 us
    unnamed x18, local copies, waits for them, and re-layouts  8.66 us

profile of v1, /device:TPU:1, one launch (start us, length us, event | category | flops | bytes accessed | tf_op | source)
XLA Modules:
  0.0 58.9 jit_solution(762171318521191628)
XLA Ops:
  0.6 0.0 copy-start
  0.6 1.4 %copy-done = bf16[1152,640]{1,0:T(8,128)(2,1)S(1)} copy-done((bf16[1152,640]{1,0:T(8,128)(2,1)S(1)}, bf16[1152,640]{1,0:T(8,128)(2,1)}, u32[]{:S(2)}) %copy-start) | copy-done | bytes 1474584
  2.0 0.0 copy-start.1
  2.0 1.4 %copy-done.1 = bf16[1152,640]{1,0:T(8,128)(2,1)S(1)} copy-done((bf16[1152,640]{1,0:T(8,128)(2,1)S(1)}, bf16[1152,640]{1,0:T(8,128)(2,1)}, u32[]{:S(2)}) %copy-start.1) | copy-done | bytes 1474584
  3.4 0.0 copy-start.2
  3.4 0.7 %copy-done.2 = bf16[8,640]{1,0:T(8,128)(2,1)S(1)} copy-done((bf16[8,640]{1,0:T(8,128)(2,1)S(1)}, bf16[8,640]{1,0:T(8,128)(2,1)}, u32[]{:S(2)}) %copy-start.2) | copy-done | bytes 10264
  4.1 0.0 copy-start.3
  4.1 0.7 %copy-done.3 = bf16[4,1152]{1,0:T(4,128)(2,1)S(1)} copy-done((bf16[4,1152]{1,0:T(4,128)(2,1)S(1)}, bf16[4,1152]{1,0:T(4,128)(2,1)}, u32[]{:S(2)}) %copy-start.3) | copy-done | bytes 9240
  4.8 0.0 copy-start.4
  4.8 0.7 %copy-done.4 = s32[2,640]{1,0:T(2,128)S(1)} copy-done((s32[2,640]{1,0:T(2,128)S(1)}, s32[2,640]{1,0:T(2,128)}, u32[]{:S(2)}) %copy-start.4) | copy-done | bytes 5144
  5.5 0.0 copy-start.5
  5.5 0.7 %copy-done.5 = bf16[4,128]{1,0:T(4,128)(2,1)S(1)} copy-done((bf16[4,128]{1,0:T(4,128)(2,1)S(1)}, bf16[4,128]{1,0:T(4,128)(2,1)}, u32[]{:S(2)}) %copy-start.5) | copy-done | bytes 1048
  6.2 0.0 copy-start.6
  6.2 0.7 %copy-done.6 = s32[2,128]{1,0:T(2,128)S(1)} copy-done((s32[2,128]{1,0:T(2,128)S(1)}, s32[2,128]{1,0:T(2,128)}, u32[]{:S(2)}) %copy-start.6) | copy-done | bytes 1048
  6.8 0.0 copy-start.7
  6.8 0.7 %copy-done.7 = s32[128]{0:T(128)S(1)} copy-done((s32[128]{0:T(128)S(1)}, s32[128]{0:T(128)}, u32[]{:S(2)}) %copy-start.7) | copy-done | bytes 536
  7.5 49.0 %shard_map.103 = (bf16[128,1152]{1,0:T(8,128)(2,1)S(1)}, bf16[1152,640]{1,0:T(8,128)(2,1)S(1)}, f32[1,128]{1,0:T(1,128)S(1)}) custom-call(bf16[8,640]{1,0:T(8,128)(2,1)S(1)} %copy-done.2, bf16[4,128]{1,0:T(4,128)(2,1)S(1)} %copy-done.5, bf16[4,1152]{1,0:T(4,128)(2,1)S(1)} %copy-done.3, bf16[1152,640]{1,0:T(8,128)(2,1)S(1)} %copy-done, ...), custom_call_target="tpu_custom_call" | custom-call | tf_op jit(solution)/shard_map/pallas_call | solution.py:211
  56.5 0.5 slice_bitcast_fusion
  57.1 0.7 %copy.13 = bf16[128,1152]{1,0:T(8,128)(2,1)} copy(bf16[128,1152]{1,0:T(8,128)(2,1)S(1)} %get-tuple-element.12) | data formatting | bytes 589824
  57.8 1.1 %copy.14 = bf16[1152,640]{1,0:T(8,128)(2,1)} copy(bf16[1152,640]{1,0:T(8,128)(2,1)S(1)} %get-tuple-element.13) | data formatting | bytes 2949120
Async XLA Ops:
  0.6 1.4 %copy-start = (bf16[1152,640]{1,0:T(8,128)(2,1)S(1)}, bf16[1152,640]{1,0:T(8,128)(2,1)}, u32[]{:S(2)}) copy-start(bf16[1152,640]{1,0:T(8,128)(2,1)} %trail_hbm.1) | copy-start | bytes 4423684
  2.0 1.4 %copy-start.1 = (bf16[1152,640]{1,0:T(8,128)(2,1)S(1)}, bf16[1152,640]{1,0:T(8,128)(2,1)}, u32[]{:S(2)}) copy-start(bf16[1152,640]{1,0:T(8,128)(2,1)} %ff_hbm.1) | copy-start | bytes 4423684
  3.4 0.7 %copy-start.2 = (bf16[8,640]{1,0:T(8,128)(2,1)S(1)}, bf16[8,640]{1,0:T(8,128)(2,1)}, u32[]{:S(2)}) copy-start(bf16[8,640]{1,0:T(8,128)(2,1)} %pf_hbm.1) | copy-start | bytes 30724
  4.1 0.7 %copy-start.3 = (bf16[4,1152]{1,0:T(4,128)(2,1)S(1)}, bf16[4,1152]{1,0:T(4,128)(2,1)}, u32[]{:S(2)}) copy-start(bf16[4,1152]{1,0:T(4,128)(2,1)} %rhs_hbm.1) | copy-start | bytes 27652
  4.8 0.7 %copy-start.4 = (s32[2,640]{1,0:T(2,128)S(1)}, s32[2,640]{1,0:T(2,128)}, u32[]{:S(2)}) copy-start(s32[2,640]{1,0:T(2,128)} %th_hbm.1) | copy-start | bytes 15364
  5.5 0.7 %copy-start.5 = (bf16[4,128]{1,0:T(4,128)(2,1)S(1)}, bf16[4,128]{1,0:T(4,128)(2,1)}, u32[]{:S(2)}) copy-start(bf16[4,128]{1,0:T(4,128)(2,1)} %dinv_hbm.1) | copy-start | bytes 3076
  6.2 0.7 %copy-start.6 = (s32[2,128]{1,0:T(2,128)S(1)}, s32[2,128]{1,0:T(2,128)}, u32[]{:S(2)}) copy-start(s32[2,128]{1,0:T(2,128)} %ph_hbm.1) | copy-start | bytes 3076
  6.8 0.7 %copy-start.7 = (s32[128]{0:T(128)S(1)}, s32[128]{0:T(128)}, u32[]{:S(2)}) copy-start(s32[128]{0:T(128)} %piv_hbm.1) | copy-start | bytes 1540

commit v2 on v1

--- a/solution.py
+++ b/solution.py
@@ -205,9 +205,22 @@
     col_copy(e_land.at[pl.ds(0, NC - 1)], e_land.at[pl.ds(0, NC - 1)], col_peer(1), 5).wait_send()
 
 
+def finish(pa_in, tu_in, eps_in, pa_out, tu_out, eps_out, sems):
+    copies = [
+        pltpu.make_async_copy(tu_in, tu_out, sems.at[0]),
+        pltpu.make_async_copy(pa_in, pa_out, sems.at[1]),
+    ]
+    for c in copies:
+        c.start()
+    eps_out[...] = eps_in[0, :72]
+    for c in copies:
+        c.wait()
+
+
 def per_device(*args):
-    anywhere = pl.BlockSpec(memory_space=pl.ANY)
+    anywhere = pl.BlockSpec(memory_space=pltpu.HBM)
     vmem = pl.BlockSpec(memory_space=pltpu.VMEM)
+    args = [pltpu.with_memory_space_constraint(a, pltpu.HBM) for a in args]
     pa, tu, eps = pl.pallas_call(
         kernel,
         out_shape=(
@@ -247,7 +260,18 @@
             collective_id=0, has_side_effects=True, vmem_limit_bytes=40 * 2**20
         ),
     )(*args)
-    return pa, tu, eps[0, :72]
+    return pl.pallas_call(
+        finish,
+        out_shape=(
+            jax.ShapeDtypeStruct((NB, SB), BF),
+            jax.ShapeDtypeStruct((SB, QB), BF),
+            jax.ShapeDtypeStruct((72,), F32),
+        ),
+        in_specs=[vmem] * 3,
+        out_specs=(anywhere, anywhere, pl.BlockSpec()),
+        scratch_shapes=[pltpu.SemaphoreType.DMA((2,))],
+        compiler_params=pltpu.CompilerParams(vmem_limit_bytes=2**20),
+    )(pa, tu, eps)
 
 
 def solution(mesh):

time: 59.2 us -> 50.9 us (0.86)
  local copies, waits for them, and re-layouts: 9.18 us -> 0 us
  Pallas kernels: 49 us -> 50.2 us
    unnamed x18 -> x0, local copies, waits for them, and re-layouts: 8.66 us -> none
    pallas_call x0 -> x1, Pallas kernels: none -> 1.73 us  [per_device(): pl.pallas_call(finish, out_shape=(jax.ShapeDtypeStruct((NB, SB), BF), jax...]
    pallas_call x1, Pallas kernels: 49 us -> 48.4 us  [per_device(): pl.pallas_call(kernel, out_shape=(jax.ShapeDtypeStruct((NB, SB), BF), jax...]
where the time goes in v2:
time: 50.9 us; the launch traced here: 50.8 us
  Pallas kernels  50.2 us (99%)
  between operations  0.64 us (1%)
    pallas_call x1, Pallas kernels, per_device(): pl.pallas_call(kernel, out_shape=(jax.ShapeDtypeStruct((NB, SB), BF), jax...  48.4 us
    pallas_call x1, Pallas kernels, per_device(): pl.pallas_call(finish, out_shape=(jax.ShapeDtypeStruct((NB, SB), BF), jax...  1.73 us

profile of v2, /device:TPU:1, one launch (start us, length us, event | category | flops | bytes accessed | tf_op | source)
XLA Modules:
  0.0 50.8 jit_solution(15908900811485680352)
XLA Ops:
  0.6 48.4 %shard_map.103 = (bf16[128,1152]{1,0:T(8,128)(2,1)S(1)}, bf16[1152,640]{1,0:T(8,128)(2,1)S(1)}, f32[1,128]{1,0:T(1,128)S(1)}) custom-call(bf16[8,640]{1,0:T(8,128)(2,1)} %pf_hbm.1, bf16[4,128]{1,0:T(4,128)(2,1)} %dinv_hbm.1, bf16[4,1152]{1,0:T(4,128)(2,1)} %rhs_hbm.1, bf16[1152,640]{1,0:T(8,128)(2,1)} %trail_hbm.1, bf16[1152,640]{1,0:T(8,128)(2,1)} %ff_hbm.1, ...), custom_call_target="tpu_custom_call" | custom-call | tf_op jit(solution)/shard_map/pallas_call | solution.py:224
  49.1 1.7 %shard_map.104 = (bf16[128,1152]{1,0:T(8,128)(2,1)}, bf16[1152,640]{1,0:T(8,128)(2,1)}, f32[72]{0:T(128)}) custom-call(bf16[128,1152]{1,0:T(8,128)(2,1)S(1)} %get-tuple-element.6.pa_in, bf16[1152,640]{1,0:T(8,128)(2,1)S(1)} %get-tuple-element.7.tu_in, f32[1,128]{1,0:T(1,128)S(1)} %get-tuple-element.8.eps_in), custom_call_target="tpu_custom_call" | custom-call | tf_op jit(solution)/shard_map/pallas_call | solution.py:263

commit v3 on v2

--- a/solution.py
+++ b/solution.py
@@ -62,10 +62,13 @@
 
     copies[0].wait()
     copies[1].wait()
-    stage[0, :, pl.ds(0, HALF)] = raw[:, pl.ds(0, HALF)]
-    stage[1, :, pl.ds(0, HALF)] = raw[:, pl.ds(SB - HALF, HALF)]
+    mine = raw[...].astype(F32)
+    inverse = mine[:, SB:]
     for h in range(2):
-        stage[h, :, pl.ds(HALF, NB)] = raw[:, pl.ds(SB, NB)]
+        at = h * (SB - HALF)
+        stage[h] = jnp.concatenate(
+            [mine[:, at : at + 384], jnp.concatenate([mine[:, at + 384 : at + HALF], inverse], axis=1)], axis=0
+        ).astype(BF)
     copies[2].wait()
 
     pl.semaphore_wait(barrier, NC - 1 + NR - 1)
@@ -111,9 +114,19 @@
         hot[pl.ds(j * QB, QB), :] = jnp.where(u_y == hy, jnp.ones((), BF), jnp.zeros((), BF))
 
     col_copy(a_land.at[pl.ds(0, NC - 1)], a_land.at[pl.ds(0, NC - 1)], col_peer(1), 0).wait_recv()
-    both = a_land[...].astype(F32).reshape(NB, HALF + NB).astype(BF)
-    mine = lax.dot_general(
-        both[:, HALF:], both[:, :HALF], (((0,), (0,)), ((), ())), preferred_element_type=F32
+    both = a_land[...].astype(F32).reshape(2 * NB, 384)
+    odd = lax.broadcasted_iota(jnp.int32, (2 * NB, NB), 0) % 8 >= 4
+    inverse = jnp.where(odd, both[:, 256:], 0.0)
+    both = both.astype(BF)
+    contract = (((0,), (0,)), ((), ()))
+    mine = jnp.concatenate(
+        [
+            lax.dot_general(
+                jnp.roll(inverse, -4, axis=0).astype(BF), both, contract, preferred_element_type=F32
+            ),
+            lax.dot_general(inverse.astype(BF), both[:, :256], contract, preferred_element_type=F32),
+        ],
+        axis=1,
     ).astype(BF)
     pa[:, pl.ds(pl.multiple_of(core * (SB - HALF), 128), HALF)] = mine
     part = pa.at[:, pl.ds(pl.multiple_of(core * HALF, 128), SB - HALF)]
@@ -166,7 +179,7 @@
         )
     grid = grid[:192] + grid[192:]
     for r in range(NR):
-        g_send[r] = grid[12 * r : 12 * r + 12]
+        g_send[r] = jnp.concatenate([grid[12 * r : 12 * r + 12], jnp.zeros((4, 256), F32)], axis=0).astype(BF)
 
     @pl.loop(1, NR)
     def _(k):
@@ -175,9 +188,9 @@
 
     d_land[row] = g_send[row]
     row_copy(d_land.at[pl.ds(0, NR - 1)], d_land.at[pl.ds(0, NR - 1)], row_peer(1), 4).wait_recv()
-    summed = d_land[0]
+    summed = d_land[0].astype(F32)
     for r in range(1, NR):
-        summed = summed + d_land[r]
+        summed = summed + d_land[r].astype(F32)
     h_lo[...] = summed[:, :128]
     h_hi[...] = summed[:, 128:]
 
@@ -207,9 +220,10 @@
 
 def finish(pa_in, tu_in, eps_in, pa_out, tu_out, eps_out, sems):
     copies = [
-        pltpu.make_async_copy(tu_in, tu_out, sems.at[0]),
-        pltpu.make_async_copy(pa_in, pa_out, sems.at[1]),
+        pltpu.make_async_copy(tu_in.at[pl.ds(k * 288, 288)], tu_out.at[pl.ds(k * 288, 288)], sems.at[k])
+        for k in range(4)
     ]
+    copies.append(pltpu.make_async_copy(pa_in, pa_out, sems.at[4]))
     for c in copies:
         c.start()
     eps_out[...] = eps_in[0, :72]
@@ -238,8 +252,8 @@
             pltpu.VMEM((2, QB), jnp.int32),
             pltpu.SMEM((NB,), jnp.int32),
             pltpu.SMEM((2, NB), jnp.int32),
-            pltpu.VMEM((2, 4, HALF + NB), BF),
-            pltpu.VMEM((NC, 4, HALF + NB), BF),
+            pltpu.VMEM((2, 8, 384), BF),
+            pltpu.VMEM((NC, 8, 384), BF),
             pltpu.VMEM((NR, 8, QB), BF),
             pltpu.VMEM((NB, SB), BF),
             pltpu.VMEM((NB, QB), F32),
@@ -247,10 +261,10 @@
             pltpu.VMEM((NR, 8, QB), BF),
             pltpu.VMEM((8 * QB, 256), BF),
             pltpu.VMEM((192, QB), BF),
-            pltpu.VMEM((NR, 12, 256), F32),
-            pltpu.VMEM((NR, 12, 256), F32),
-            pltpu.VMEM((12, 128), F32),
-            pltpu.VMEM((12, 128), F32),
+            pltpu.VMEM((NR, 16, 256), BF),
+            pltpu.VMEM((NR, 16, 256), BF),
+            pltpu.VMEM((16, 128), F32),
+            pltpu.VMEM((16, 128), F32),
             pltpu.VMEM((NC, 1, 128), F32),
             pltpu.VMEM((NC, 1, 128), F32),
             pltpu.SemaphoreType.DMA((8,)),
@@ -269,7 +283,7 @@
         ),
         in_specs=[vmem] * 3,
         out_specs=(anywhere, anywhere, pl.BlockSpec()),
-        scratch_shapes=[pltpu.SemaphoreType.DMA((2,))],
+        scratch_shapes=[pltpu.SemaphoreType.DMA((5,))],
         compiler_params=pltpu.CompilerParams(vmem_limit_bytes=2**20),
     )(pa, tu, eps)
 

time: 50.9 us -> 49.1 us (0.965)
  Pallas kernels: 50.2 us -> 48.3 us
    pallas_call x1, Pallas kernels: 48.4 us -> 46.6 us  [per_device(): pl.pallas_call(kernel, out_shape=(jax.ShapeDtypeStruct((NB, SB), BF), jax...]
where the time goes in v3:
time: 49.1 us; the launch traced here: 49 us
  Pallas kernels  48.3 us (98%)
  between operations  0.64 us (1%)
    pallas_call x1, Pallas kernels, per_device(): pl.pallas_call(kernel, out_shape=(jax.ShapeDtypeStruct((NB, SB), BF), jax...  46.6 us
    pallas_call x1, Pallas kernels, per_device(): pl.pallas_call(finish, out_shape=(jax.ShapeDtypeStruct((NB, SB), BF), jax...  1.76 us

profile of v3, /device:TPU:1, one launch (start us, length us, event | category | flops | bytes accessed | tf_op | source)
XLA Modules:
  0.0 49.0 jit_solution(14397728182443185812)
XLA Ops:
  0.6 46.6 %shard_map.103 = (bf16[128,1152]{1,0:T(8,128)(2,1)S(1)}, bf16[1152,640]{1,0:T(8,128)(2,1)S(1)}, f32[1,128]{1,0:T(1,128)S(1)}) custom-call(bf16[8,640]{1,0:T(8,128)(2,1)} %pf_hbm.1, bf16[4,128]{1,0:T(4,128)(2,1)} %dinv_hbm.1, bf16[4,1152]{1,0:T(4,128)(2,1)} %rhs_hbm.1, bf16[1152,640]{1,0:T(8,128)(2,1)} %trail_hbm.1, bf16[1152,640]{1,0:T(8,128)(2,1)} %ff_hbm.1, ...), custom_call_target="tpu_custom_call" | custom-call | tf_op jit(solution)/shard_map/pallas_call | solution.py:238
  47.2 1.8 %shard_map.104 = (bf16[128,1152]{1,0:T(8,128)(2,1)}, bf16[1152,640]{1,0:T(8,128)(2,1)}, f32[72]{0:T(128)}) custom-call(bf16[128,1152]{1,0:T(8,128)(2,1)S(1)} %get-tuple-element.6.pa_in, bf16[1152,640]{1,0:T(8,128)(2,1)S(1)} %get-tuple-element.7.tu_in, f32[1,128]{1,0:T(1,128)S(1)} %get-tuple-element.8.eps_in), custom_call_target="tpu_custom_call" | custom-call | tf_op jit(solution)/shard_map/pallas_call | solution.py:277

commit v4 on v3

--- a/solution.py
+++ b/solution.py
@@ -16,6 +16,8 @@
 QB = 640
 HALF = 640
 MESH = pl.DeviceIdType.MESH
+COL_ORDER = [z * 4 + q for z in (4, 7, 3, 5, 6, 2, 1, 0) for q in range(4) if z + q > 0]
+ROW_ORDER = [y * 4 + x for y in (2, 3, 1, 0) for x in (2, 3, 1, 0) if y + x > 0]
 BF = jnp.bfloat16
 F32 = jnp.float32
 
@@ -31,12 +33,6 @@
     col = lax.axis_index("col")
     core = col % 2
 
-    def row_peer(k):
-        return (row + k) % NR
-
-    def col_peer(k):
-        return (col + k) % NC
-
     copies = [
         pltpu.make_async_copy(rhs_hbm, raw.at[:, pl.ds(0, SB)], loc.at[0]),
         pltpu.make_async_copy(dinv_hbm, raw.at[:, pl.ds(SB, NB)], loc.at[1]),
@@ -47,18 +43,16 @@
         pltpu.make_async_copy(ff_hbm, ff_v, loc.at[6]),
         pltpu.make_async_copy(trail_hbm, trail_v, loc.at[7]),
     ]
-    for c in copies:
+    for c in copies[:2]:
         c.start()
 
     barrier = pltpu.get_barrier_semaphore()
-
-    @pl.loop(1, NC)
-    def _(k):
-        pl.semaphore_signal(barrier, inc=1, device_id=(row, col_peer(k)), device_id_type=MESH)
-
-    @pl.loop(1, NR)
-    def _(k):
-        pl.semaphore_signal(barrier, inc=1, device_id=(row_peer(k), col), device_id_type=MESH)
+    for k in COL_ORDER:
+        pl.semaphore_signal(barrier, inc=1, device_id=(row, col ^ k), device_id_type=MESH)
+    for k in ROW_ORDER:
+        pl.semaphore_signal(barrier, inc=1, device_id=(row ^ k, col), device_id_type=MESH)
+    for c in copies[2:]:
+        c.start()
 
     copies[0].wait()
     copies[1].wait()
@@ -69,8 +63,6 @@
         stage[h] = jnp.concatenate(
             [mine[:, at : at + 384], jnp.concatenate([mine[:, at + 384 : at + HALF], inverse], axis=1)], axis=0
         ).astype(BF)
-    copies[2].wait()
-
     pl.semaphore_wait(barrier, NC - 1 + NR - 1)
 
     def col_copy(src, dst, target, k):
@@ -85,14 +77,12 @@
             device_id=(target, col), device_id_type=MESH,
         )
 
-    @pl.loop(1, NC)
-    def _(k):
-        target = col_peer(k)
+    for k in COL_ORDER:
+        target = col ^ k
         col_copy(stage.at[target % 2], a_land.at[col], target, 0).start()
-
-    @pl.loop(1, NR)
-    def _(k):
-        row_copy(pf_v, b_land.at[row], row_peer(k), 1).start()
+    copies[2].wait()
+    for k in ROW_ORDER:
+        row_copy(pf_v, b_land.at[row], row ^ k, 1).start()
 
     a_land[col] = stage[core]
     b_land[row] = pf_v[...]
@@ -113,7 +103,7 @@
         hy = ph_s[1, unpivoted].astype(F32).astype(BF)
         hot[pl.ds(j * QB, QB), :] = jnp.where(u_y == hy, jnp.ones((), BF), jnp.zeros((), BF))
 
-    col_copy(a_land.at[pl.ds(0, NC - 1)], a_land.at[pl.ds(0, NC - 1)], col_peer(1), 0).wait_recv()
+    col_copy(a_land.at[pl.ds(0, NC - 1)], a_land.at[pl.ds(0, NC - 1)], col ^ 1, 0).wait_recv()
     both = a_land[...].astype(F32).reshape(2 * NB, 384)
     odd = lax.broadcasted_iota(jnp.int32, (2 * NB, NB), 0) % 8 >= 4
     inverse = jnp.where(odd, both[:, 256:], 0.0)
@@ -130,20 +120,22 @@
     ).astype(BF)
     pa[:, pl.ds(pl.multiple_of(core * (SB - HALF), 128), HALF)] = mine
     part = pa.at[:, pl.ds(pl.multiple_of(core * HALF, 128), SB - HALF)]
-    swap = col_copy(part, part, col + 1 - 2 * core, 2)
+    swap = col_copy(part, part, col ^ 1, 2)
     swap.start()
     copies[6].wait()
+    own_rows = pl.ds(pl.multiple_of(core * (SB - HALF), 128), HALF)
+    corr[...] = jnp.dot(mine, ff_v[own_rows, :], preferred_element_type=F32)
     swap.wait()
 
-    corr[...] = jnp.dot(pa[...], ff_v[...], preferred_element_type=F32)
+    other = pl.ds(pl.multiple_of((1 - core) * HALF, 128), SB - HALF)
+    corr[...] += jnp.dot(pa[:, other], ff_v[other, :], preferred_element_type=F32)
     c_send[...] = corr[...].reshape(NR, 8, QB).astype(BF)
 
-    @pl.loop(1, NR)
-    def _(k):
-        target = row_peer(k)
+    for k in ROW_ORDER:
+        target = row ^ k
         row_copy(c_send.at[target], c_land.at[row], target, 3).start()
 
-    row_copy(b_land.at[pl.ds(0, NR - 1)], b_land.at[pl.ds(0, NR - 1)], row_peer(1), 1).wait_recv()
+    row_copy(b_land.at[pl.ds(0, NR - 1)], b_land.at[pl.ds(0, NR - 1)], row ^ 1, 1).wait_recv()
     factor = b_land[...].astype(F32).reshape(NB, QB).astype(BF)
     copies[7].wait()
     for t in range(3):
@@ -154,7 +146,7 @@
         tu_out[at, :] = (trail_v[at, :].astype(F32) - update).astype(BF)
     pa_out[...] = pa[...]
 
-    row_copy(c_land.at[pl.ds(0, NR - 1)], c_land.at[pl.ds(0, NR - 1)], row_peer(1), 3).wait_recv()
+    row_copy(c_land.at[pl.ds(0, NR - 1)], c_land.at[pl.ds(0, NR - 1)], row ^ 1, 3).wait_recv()
     total = corr[pl.ds(pl.multiple_of(row * 8, 8), 8), :]
     for r in range(NR):
         total = total + c_land[r].astype(F32)
@@ -181,13 +173,12 @@
     for r in range(NR):
         g_send[r] = jnp.concatenate([grid[12 * r : 12 * r + 12], jnp.zeros((4, 256), F32)], axis=0).astype(BF)
 
-    @pl.loop(1, NR)
-    def _(k):
-        target = row_peer(k)
+    for k in ROW_ORDER:
+        target = row ^ k
         row_copy(g_send.at[target], d_land.at[row], target, 4).start()
 
     d_land[row] = g_send[row]
-    row_copy(d_land.at[pl.ds(0, NR - 1)], d_land.at[pl.ds(0, NR - 1)], row_peer(1), 4).wait_recv()
+    row_copy(d_land.at[pl.ds(0, NR - 1)], d_land.at[pl.ds(0, NR - 1)], row ^ 1, 4).wait_recv()
     summed = d_land[0].astype(F32)
     for r in range(1, NR):
         summed = summed + d_land[r].astype(F32)
@@ -202,31 +193,31 @@
         for g in range(4):
             e_send[8 * g + h] = piece[g : g + 1]
 
-    @pl.loop(1, NC)
-    def _(k):
-        target = col_peer(k)
+    for k in COL_ORDER:
+        target = col ^ k
         col_copy(e_send.at[target], e_land.at[col], target, 5).start()
 
     e_land[col] = e_send[col]
-    col_copy(e_land.at[pl.ds(0, NC - 1)], e_land.at[pl.ds(0, NC - 1)], col_peer(1), 5).wait_recv()
+    col_copy(e_land.at[pl.ds(0, NC - 1)], e_land.at[pl.ds(0, NC - 1)], col ^ 1, 5).wait_recv()
     eps_out[...] = jnp.sum(e_land[...], axis=0) * F32(1.0 / math.sqrt(S * NB))
 
-    col_copy(a_land.at[pl.ds(0, NC - 1)], a_land.at[pl.ds(0, NC - 1)], col_peer(1), 0).wait_send()
-    row_copy(b_land.at[pl.ds(0, NR - 1)], b_land.at[pl.ds(0, NR - 1)], row_peer(1), 1).wait_send()
-    row_copy(c_land.at[pl.ds(0, NR - 1)], c_land.at[pl.ds(0, NR - 1)], row_peer(1), 3).wait_send()
-    row_copy(d_land.at[pl.ds(0, NR - 1)], d_land.at[pl.ds(0, NR - 1)], row_peer(1), 4).wait_send()
-    col_copy(e_land.at[pl.ds(0, NC - 1)], e_land.at[pl.ds(0, NC - 1)], col_peer(1), 5).wait_send()
-
-
-def finish(pa_in, tu_in, eps_in, pa_out, tu_out, eps_out, sems):
+    col_copy(a_land.at[pl.ds(0, NC - 1)], a_land.at[pl.ds(0, NC - 1)], col ^ 1, 0).wait_send()
+    row_copy(b_land.at[pl.ds(0, NR - 1)], b_land.at[pl.ds(0, NR - 1)], row ^ 1, 1).wait_send()
+    row_copy(c_land.at[pl.ds(0, NR - 1)], c_land.at[pl.ds(0, NR - 1)], row ^ 1, 3).wait_send()
+    row_copy(d_land.at[pl.ds(0, NR - 1)], d_land.at[pl.ds(0, NR - 1)], row ^ 1, 4).wait_send()
+    col_copy(e_land.at[pl.ds(0, NC - 1)], e_land.at[pl.ds(0, NC - 1)], col ^ 1, 5).wait_send()
+
+
+def finish(pa_in, tu_in, eps_in, pa_out, tu_out, eps_out, eps_v, sems):
+    eps_v[...] = eps_in[0, :72]
     copies = [
         pltpu.make_async_copy(tu_in.at[pl.ds(k * 288, 288)], tu_out.at[pl.ds(k * 288, 288)], sems.at[k])
         for k in range(4)
     ]
     copies.append(pltpu.make_async_copy(pa_in, pa_out, sems.at[4]))
+    copies.append(pltpu.make_async_copy(eps_v, eps_out, sems.at[5]))
     for c in copies:
         c.start()
-    eps_out[...] = eps_in[0, :72]
     for c in copies:
         c.wait()
 
@@ -282,8 +273,8 @@
             jax.ShapeDtypeStruct((72,), F32),
         ),
         in_specs=[vmem] * 3,
-        out_specs=(anywhere, anywhere, pl.BlockSpec()),
-        scratch_shapes=[pltpu.SemaphoreType.DMA((5,))],
+        out_specs=(anywhere,) * 3,
+        scratch_shapes=[pltpu.VMEM((72,), F32), pltpu.SemaphoreType.DMA((6,))],
         compiler_params=pltpu.CompilerParams(vmem_limit_bytes=2**20),
     )(pa, tu, eps)
 

time: 49.1 us -> 46.6 us (0.949)
  Pallas kernels: 48.3 us -> 45.8 us
    pallas_call x1, Pallas kernels: 46.6 us -> 44.5 us  [per_device(): pl.pallas_call(kernel, out_shape=(jax.ShapeDtypeStruct((NB, SB), BF), jax...]
    pallas_call x1, Pallas kernels: 1.76 us -> 1.26 us  [per_device(): pl.pallas_call(finish, out_shape=(jax.ShapeDtypeStruct((NB, SB), BF), jax...]
where the time goes in v4:
time: 46.6 us; the launch traced here: 46.4 us
  Pallas kernels  45.8 us (98%)
  between operations  0.64 us (1%)
    pallas_call x1, Pallas kernels, per_device(): pl.pallas_call(kernel, out_shape=(jax.ShapeDtypeStruct((NB, SB), BF), jax...  44.5 us
    pallas_call x1, Pallas kernels, per_device(): pl.pallas_call(finish, out_shape=(jax.ShapeDtypeStruct((NB, SB), BF), jax...  1.26 us

profile of v4, /device:TPU:1, one launch (start us, length us, event | category | flops | bytes accessed | tf_op | source)
XLA Modules:
  0.0 46.4 jit_solution(13200004507940905323)
XLA Ops:
  0.6 44.5 %shard_map.103 = (bf16[128,1152]{1,0:T(8,128)(2,1)S(1)}, bf16[1152,640]{1,0:T(8,128)(2,1)S(1)}, f32[1,128]{1,0:T(1,128)S(1)}) custom-call(bf16[8,640]{1,0:T(8,128)(2,1)} %pf_hbm.1, bf16[4,128]{1,0:T(4,128)(2,1)} %dinv_hbm.1, bf16[4,1152]{1,0:T(4,128)(2,1)} %rhs_hbm.1, bf16[1152,640]{1,0:T(8,128)(2,1)} %trail_hbm.1, bf16[1152,640]{1,0:T(8,128)(2,1)} %ff_hbm.1, ...), custom_call_target="tpu_custom_call" | custom-call | tf_op jit(solution)/shard_map/pallas_call | solution.py:229
  45.1 1.3 %shard_map.104 = (bf16[128,1152]{1,0:T(8,128)(2,1)}, bf16[1152,640]{1,0:T(8,128)(2,1)}, f32[72]{0:T(128)}) custom-call(bf16[128,1152]{1,0:T(8,128)(2,1)S(1)} %get-tuple-element.6.pa_in, bf16[1152,640]{1,0:T(8,128)(2,1)S(1)} %get-tuple-element.7.tu_in, f32[1,128]{1,0:T(1,128)S(1)} %get-tuple-element.8.eps_in), custom_call_target="tpu_custom_call" | custom-call | tf_op jit(solution)/shard_map/pallas_call | solution.py:268

commit v5 on v4

--- a/solution.py
+++ b/solution.py
@@ -32,6 +32,7 @@
     row = lax.axis_index("row")
     col = lax.axis_index("col")
     core = col % 2
+    chip = col // 2
 
     copies = [
         pltpu.make_async_copy(rhs_hbm, raw.at[:, pl.ds(0, SB)], loc.at[0]),
@@ -43,7 +44,7 @@
         pltpu.make_async_copy(ff_hbm, ff_v, loc.at[6]),
         pltpu.make_async_copy(trail_hbm, trail_v, loc.at[7]),
     ]
-    for c in copies[:2]:
+    for c in copies[:3]:
         c.start()
 
     barrier = pltpu.get_barrier_semaphore()
@@ -51,18 +52,13 @@
         pl.semaphore_signal(barrier, inc=1, device_id=(row, col ^ k), device_id_type=MESH)
     for k in ROW_ORDER:
         pl.semaphore_signal(barrier, inc=1, device_id=(row ^ k, col), device_id_type=MESH)
-    for c in copies[2:]:
-        c.start()
 
     copies[0].wait()
     copies[1].wait()
     mine = raw[...].astype(F32)
-    inverse = mine[:, SB:]
-    for h in range(2):
-        at = h * (SB - HALF)
-        stage[h] = jnp.concatenate(
-            [mine[:, at : at + 384], jnp.concatenate([mine[:, at + 384 : at + HALF], inverse], axis=1)], axis=0
-        ).astype(BF)
+    own = jnp.concatenate([mine[:, :HALF], mine[:, HALF:]], axis=0).astype(BF)
+    stage[...] = own
+
     pl.semaphore_wait(barrier, NC - 1 + NR - 1)
 
     def col_copy(src, dst, target, k):
@@ -78,13 +74,15 @@
         )
 
     for k in COL_ORDER:
-        target = col ^ k
-        col_copy(stage.at[target % 2], a_land.at[col], target, 0).start()
+        if k % 2 == 0:
+            col_copy(stage, a_land.at[core, chip], col ^ k, 0).start()
+    for c in copies[3:]:
+        c.start()
     copies[2].wait()
     for k in ROW_ORDER:
         row_copy(pf_v, b_land.at[row], row ^ k, 1).start()
 
-    a_land[col] = stage[core]
+    a_land[core, chip] = own
     b_land[row] = pf_v[...]
     c_land[row] = jnp.zeros((8, QB), BF)
 
@@ -103,32 +101,33 @@
         hy = ph_s[1, unpivoted].astype(F32).astype(BF)
         hot[pl.ds(j * QB, QB), :] = jnp.where(u_y == hy, jnp.ones((), BF), jnp.zeros((), BF))
 
-    col_copy(a_land.at[pl.ds(0, NC - 1)], a_land.at[pl.ds(0, NC - 1)], col ^ 1, 0).wait_recv()
-    both = a_land[...].astype(F32).reshape(2 * NB, 384)
-    odd = lax.broadcasted_iota(jnp.int32, (2 * NB, NB), 0) % 8 >= 4
-    inverse = jnp.where(odd, both[:, 256:], 0.0)
-    both = both.astype(BF)
-    contract = (((0,), (0,)), ((), ()))
-    mine = jnp.concatenate(
-        [
-            lax.dot_general(
-                jnp.roll(inverse, -4, axis=0).astype(BF), both, contract, preferred_element_type=F32
-            ),
-            lax.dot_general(inverse.astype(BF), both[:, :256], contract, preferred_element_type=F32),
-        ],
-        axis=1,
-    ).astype(BF)
-    pa[:, pl.ds(pl.multiple_of(core * (SB - HALF), 128), HALF)] = mine
-    part = pa.at[:, pl.ds(pl.multiple_of(core * HALF, 128), SB - HALF)]
+    col_copy(a_land.at[0, pl.ds(0, NC // 2 - 1)], a_land.at[0, pl.ds(0, NC // 2 - 1)], col ^ 1, 0).wait_recv()
+    part = a_land.at[core]
     swap = col_copy(part, part, col ^ 1, 2)
     swap.start()
+    odd = lax.broadcasted_iota(jnp.int32, (NB, NB), 0) % 8 >= 4
+    contract = (((0,), (0,)), ((), ()))
+
+    def terms(block):
+        wide = block.astype(F32).reshape(NB, HALF)
+        inverse = jnp.where(odd, wide[:, SB - HALF :], 0.0)
+        wide = wide.astype(BF)
+        return (
+            lax.dot_general(
+                jnp.roll(inverse, -4, axis=0).astype(BF), wide, contract, preferred_element_type=F32
+            ),
+            lax.dot_general(
+                inverse.astype(BF), wide[:, : SB - HALF], contract, preferred_element_type=F32
+            ),
+        )
+
+    near = terms(a_land[core])
     copies[6].wait()
-    own_rows = pl.ds(pl.multiple_of(core * (SB - HALF), 128), HALF)
-    corr[...] = jnp.dot(mine, ff_v[own_rows, :], preferred_element_type=F32)
     swap.wait()
-
-    other = pl.ds(pl.multiple_of((1 - core) * HALF, 128), SB - HALF)
-    corr[...] += jnp.dot(pa[:, other], ff_v[other, :], preferred_element_type=F32)
+    far = terms(a_land[1 - core])
+    pa[:, pl.ds(0, HALF)] = (near[0] + far[0]).astype(BF)
+    pa[:, pl.ds(HALF, SB - HALF)] = (near[1] + far[1]).astype(BF)
+    corr[...] = jnp.dot(pa[...], ff_v[...], preferred_element_type=F32)
     c_send[...] = corr[...].reshape(NR, 8, QB).astype(BF)
 
     for k in ROW_ORDER:
@@ -201,7 +200,7 @@
     col_copy(e_land.at[pl.ds(0, NC - 1)], e_land.at[pl.ds(0, NC - 1)], col ^ 1, 5).wait_recv()
     eps_out[...] = jnp.sum(e_land[...], axis=0) * F32(1.0 / math.sqrt(S * NB))
 
-    col_copy(a_land.at[pl.ds(0, NC - 1)], a_land.at[pl.ds(0, NC - 1)], col ^ 1, 0).wait_send()
+    col_copy(a_land.at[0, pl.ds(0, NC // 2 - 1)], a_land.at[0, pl.ds(0, NC // 2 - 1)], col ^ 1, 0).wait_send()
     row_copy(b_land.at[pl.ds(0, NR - 1)], b_land.at[pl.ds(0, NR - 1)], row ^ 1, 1).wait_send()
     row_copy(c_land.at[pl.ds(0, NR - 1)], c_land.at[pl.ds(0, NR - 1)], row ^ 1, 3).wait_send()
     row_copy(d_land.at[pl.ds(0, NR - 1)], d_land.at[pl.ds(0, NR - 1)], row ^ 1, 4).wait_send()
@@ -243,8 +242,8 @@
             pltpu.VMEM((2, QB), jnp.int32),
             pltpu.SMEM((NB,), jnp.int32),
             pltpu.SMEM((2, NB), jnp.int32),
-            pltpu.VMEM((2, 8, 384), BF),
-            pltpu.VMEM((NC, 8, 384), BF),
+            pltpu.VMEM((8, HALF), BF),
+            pltpu.VMEM((2, NC // 2, 8, HALF), BF),
             pltpu.VMEM((NR, 8, QB), BF),
             pltpu.VMEM((NB, SB), BF),
             pltpu.VMEM((NB, QB), F32),

time: 46.6 us -> 46.1 us (0.989)
  Pallas kernels: 45.8 us -> 45.3 us
where the time goes in v5:
time: 46.1 us; the launch traced here: 45.9 us
  Pallas kernels  45.3 us (98%)
  between operations  0.64 us (1%)
    pallas_call x1, Pallas kernels, per_device(): pl.pallas_call(kernel, out_shape=(jax.ShapeDtypeStruct((NB, SB), BF), jax...  44 us
    pallas_call x1, Pallas kernels, per_device(): pl.pallas_call(finish, out_shape=(jax.ShapeDtypeStruct((NB, SB), BF), jax...  1.26 us

profile of v5, /device:TPU:1, one launch (start us, length us, event | category | flops | bytes accessed | tf_op | source)
XLA Modules:
  0.0 45.9 jit_solution(14341304113267883896)
XLA Ops:
  0.6 44.0 %shard_map.103 = (bf16[128,1152]{1,0:T(8,128)(2,1)S(1)}, bf16[1152,640]{1,0:T(8,128)(2,1)S(1)}, f32[1,128]{1,0:T(1,128)S(1)}) custom-call(bf16[8,640]{1,0:T(8,128)(2,1)} %pf_hbm.1, bf16[4,128]{1,0:T(4,128)(2,1)} %dinv_hbm.1, bf16[4,1152]{1,0:T(4,128)(2,1)} %rhs_hbm.1, bf16[1152,640]{1,0:T(8,128)(2,1)} %trail_hbm.1, bf16[1152,640]{1,0:T(8,128)(2,1)} %ff_hbm.1, ...), custom_call_target="tpu_custom_call" | custom-call | tf_op jit(solution)/shard_map/pallas_call | solution.py:228
  44.7 1.3 %shard_map.104 = (bf16[128,1152]{1,0:T(8,128)(2,1)}, bf16[1152,640]{1,0:T(8,128)(2,1)}, f32[72]{0:T(128)}) custom-call(bf16[128,1152]{1,0:T(8,128)(2,1)S(1)} %get-tuple-element.6.pa_in, bf16[1152,640]{1,0:T(8,128)(2,1)S(1)} %get-tuple-element.7.tu_in, f32[1,128]{1,0:T(1,128)S(1)} %get-tuple-element.8.eps_in), custom_call_target="tpu_custom_call" | custom-call | tf_op jit(solution)/shard_map/pallas_call | solution.py:267

commit v6 on v5

--- a/solution.py
+++ b/solution.py
@@ -170,7 +170,9 @@
         )
     grid = grid[:192] + grid[192:]
     for r in range(NR):
-        g_send[r] = jnp.concatenate([grid[12 * r : 12 * r + 12], jnp.zeros((4, 256), F32)], axis=0).astype(BF)
+        block = grid[12 * r : 12 * r + 12]
+        tail = jnp.concatenate([block[:6, 128:192], block[6:, 128:192]], axis=1)
+        g_send[r] = jnp.concatenate([block[:, :128], tail, jnp.zeros((6, 128), F32)], axis=0).astype(BF)
 
     for k in ROW_ORDER:
         target = row ^ k
@@ -181,8 +183,9 @@
     summed = d_land[0].astype(F32)
     for r in range(1, NR):
         summed = summed + d_land[r].astype(F32)
-    h_lo[...] = summed[:, :128]
-    h_hi[...] = summed[:, 128:]
+    h_lo[...] = summed[:16]
+    tail = jnp.concatenate([summed[12:18, :64], summed[12:18, 64:], jnp.zeros((4, 64), F32)], axis=0)
+    h_hi[...] = jnp.concatenate([tail, jnp.zeros((16, 64), F32)], axis=1)
 
     flat = jnp.concatenate(
         [piece for t in range(3) for piece in (h_lo[pl.ds(t, 4, 3), :], h_hi[pl.ds(t, 4, 3), :][:, :64])], axis=1
@@ -251,8 +254,8 @@
             pltpu.VMEM((NR, 8, QB), BF),
             pltpu.VMEM((8 * QB, 256), BF),
             pltpu.VMEM((192, QB), BF),
-            pltpu.VMEM((NR, 16, 256), BF),
-            pltpu.VMEM((NR, 16, 256), BF),
+            pltpu.VMEM((NR, 24, 128), BF),
+            pltpu.VMEM((NR, 24, 128), BF),
             pltpu.VMEM((16, 128), F32),
             pltpu.VMEM((16, 128), F32),
             pltpu.VMEM((NC, 1, 128), F32),

time: 46.1 us -> 46.1 us (level)
  no operation moved by 1% of the time
where the time goes in v6:
time: 46.1 us; the launch traced here: 45.9 us
  Pallas kernels  45.3 us (98%)
  between operations  0.64 us (1%)
    pallas_call x1, Pallas kernels, per_device(): pl.pallas_call(kernel, out_shape=(jax.ShapeDtypeStruct((NB, SB), BF), jax...  44 us
    pallas_call x1, Pallas kernels, per_device(): pl.pallas_call(finish, out_shape=(jax.ShapeDtypeStruct((NB, SB), BF), jax...  1.26 us

profile of v6, /device:TPU:1, one launch (start us, length us, event | category | flops | bytes accessed | tf_op | source)
XLA Modules:
  0.0 45.9 jit_solution(6994375972994839382)
XLA Ops:
  0.6 44.0 %shard_map.103 = (bf16[128,1152]{1,0:T(8,128)(2,1)S(1)}, bf16[1152,640]{1,0:T(8,128)(2,1)S(1)}, f32[1,128]{1,0:T(1,128)S(1)}) custom-call(bf16[8,640]{1,0:T(8,128)(2,1)} %pf_hbm.1, bf16[4,128]{1,0:T(4,128)(2,1)} %dinv_hbm.1, bf16[4,1152]{1,0:T(4,128)(2,1)} %rhs_hbm.1, bf16[1152,640]{1,0:T(8,128)(2,1)} %trail_hbm.1, bf16[1152,640]{1,0:T(8,128)(2,1)} %ff_hbm.1, ...), custom_call_target="tpu_custom_call" | custom-call | tf_op jit(solution)/shard_map/pallas_call | solution.py:231
  44.6 1.3 %shard_map.104 = (bf16[128,1152]{1,0:T(8,128)(2,1)}, bf16[1152,640]{1,0:T(8,128)(2,1)}, f32[72]{0:T(128)}) custom-call(bf16[128,1152]{1,0:T(8,128)(2,1)S(1)} %get-tuple-element.6.pa_in, bf16[1152,640]{1,0:T(8,128)(2,1)S(1)} %get-tuple-element.7.tu_in, f32[1,128]{1,0:T(1,128)S(1)} %get-tuple-element.8.eps_in), custom_call_target="tpu_custom_call" | custom-call | tf_op jit(solution)/shard_map/pallas_call | solution.py:270
